TPU v7x, 32 devices: a whole 2x2x4 slice. The times are simulated.
32 devices in a mesh: surf: 8 (over z, y), depth: 4 (over x, core).
Axes of the slice: x: 2, y: 2, z: 4, core: 2. Of those that a mesh axis runs over, the one named last changes fastest.
Arguments:
- wave_now: float32 [4, 64, 64, 128], P(None, 'surf', 'depth'), may hold values from -6 to 6
- wave_old: float32 [4, 64, 64, 128], P(None, 'surf', 'depth'), may hold values from -6 to 6
- adj_now: float32 [4, 64, 64, 128], P(None, 'surf', 'depth'), may hold values from -6 to 6
- adj_old: float32 [4, 64, 64, 128], P(None, 'surf', 'depth'), may hold values from -6 to 6
- source: float32 [4, 64, 64, 128], P(None, 'surf', 'depth'), may hold values from -24 to 24
- adj_source: float32 [4, 64, 64, 128], P(None, 'surf', 'depth'), may hold values from -24 to 24
- inv_density: float32 [125, 8192], P(None, ('surf', 'depth')), may hold values from 0.5 to 1.5
- inv_modulus: float32 [125, 8192], P(None, ('surf', 'depth')), may hold values from 0.5 to 1.5
- element_cell: int32 [32, 256], P(('surf', 'depth')), may hold values from 0 to 255, as said below
- send_elem: int32 [32, 4, 256], P(('surf', 'depth')), may hold values from 0 to 255, as said below
- send_brick: int32 [32, 4, 256], P(('surf', 'depth')), may hold values from 0 to 1023, as said below
- send_count: int32 [32, 4], P(('surf', 'depth')), may hold values from 0 to 256, as said below
Outputs:
- wave_next: float32 [4, 64, 64, 128], P(None, 'surf', 'depth')
- adj_next: float32 [4, 64, 64, 128], P(None, 'surf', 'depth')
- brick_kernel: float32 [125, 32768], P(None, ('surf', 'depth'))
Inputs may be any that keep to these rules, and one draw needn't show every extreme that they name: Each row of element_cell is a permutation of the cells of one device. `send_elem`: row t of device k lists in its first send_count[k, t] slots the stored elements of device k whose blocks go to row t's device; over the four rows of a device each of its elements is listed exactly once; other slots hold 0. `send_brick`: in live slots the receiving brick within the receiving device; other slots hold 0. `send_count`: A device's counts sum to 256; rows 1 and 3 of devices with the last surf index, and rows 2 and 3 of devices with the last depth index, are empty; in every draw the device with the last surf and depth index fills row 0 with all 256 slots.
All inputs are finite; a program needn't handle non-finite values.
Results may differ from a plain program's by a relative error of at most 0.0003.
Values sent between devices are 32-bit elements; how exact they have to be, the bound alone decides.
A program may use at most 128 MiB of HBM per device.

v0:
```python
import functools
import math

import jax
import jax.numpy as jnp
import numpy as np
from jax import lax
from jax.experimental import pallas as pl
from jax.experimental.pallas import tpu as pltpu
from jax.sharding import PartitionSpec as P

time_step = 0.05
precise = lax.Precision.HIGHEST
MESH = pl.DeviceIdType.MESH
f32 = jnp.float32
bf16 = jnp.bfloat16

NODES_A, NODES_C, NODES_B = 8, 16, 128
PLANE = NODES_A * NODES_C
BLOCK_ROWS = 144
FACE_A, FACE_C, FACE_D = 144, 72, 16


def gll_numbers():
    points = np.array([-1.0, -math.sqrt(3.0 / 7.0), 0.0, math.sqrt(3.0 / 7.0), 1.0])
    weights = np.array([0.1, 49.0 / 90.0, 32.0 / 45.0, 49.0 / 90.0, 0.1])
    identity = np.eye(5)
    on_diagonal = identity > 0.5
    differences = points[:, None] - points[None, :] + identity
    products = np.prod(differences, axis=1)
    derivative = products[:, None] / products[None, :] / differences
    inverse = np.where(on_diagonal, 0.0, 1.0 / differences)
    derivative = np.where(on_diagonal, inverse.sum(axis=1)[:, None], derivative)
    return derivative, weights


D, W = gll_numbers()


def tables():
    spread = np.zeros((512, 640), np.float32)
    for ec in range(4):
        for eb in range(32):
            for r in range(5):
                spread[ec * 128 + (4 * eb + r) % 128, r * 128 + ec * 32 + eb] = 1.0
    expand = np.zeros((1000, 128), np.float32)
    expand[np.arange(1000), np.arange(1000) // 8] = 1.0
    gather = np.zeros((128, 1024), np.float32)
    gather[np.arange(1000) // 8, np.arange(1000)] = 0.5
    select = np.zeros((480, 128), np.float32)
    for r in range(5):
        for ea in range(2):
            for p in range(5):
                for q in range(5):
                    select[(r * 2 + ea) * 48 + (4 * ea + p) * 5 + q, p * 25 + q * 5 + r] = 1.0
    cubature = (W[:, None, None] * W[None, :, None] * W[None, None, :]).reshape(-1)
    scale = np.zeros((128, 128), np.float32)
    scale[:125] = cubature[:, None]
    return (spread, spread.T.copy(), expand, gather, select), scale


def two_terms(x):
    high = x.astype(bf16)
    return high, (x - high.astype(f32)).astype(bf16)


def dot_left(x, table):
    high, low = two_terms(x)
    return jnp.dot(high, table, preferred_element_type=f32) + jnp.dot(
        low, table, preferred_element_type=f32
    )


def dot_right(table, x):
    high, low = two_terms(x)
    return jnp.dot(table, high, preferred_element_type=f32) + jnp.dot(
        table, low, preferred_element_type=f32
    )


def dot_rows(x, table):
    return lax.dot_general(x, table, (((1,), (1,)), ((), ())), preferred_element_type=f32)


def forward(v):
    s0, s1, d0, d1 = v[0] + v[4], v[1] + v[3], v[0] - v[4], v[1] - v[3]
    out = [None] * 5
    for i in range(2):
        even = (
            float((D[i, 0] + D[i, 4]) / 2) * s0
            + float((D[i, 1] + D[i, 3]) / 2) * s1
            + float(D[i, 2]) * v[2]
        )
        odd = float((D[i, 0] - D[i, 4]) / 2) * d0 + float((D[i, 1] - D[i, 3]) / 2) * d1
        out[i] = even + odd
        out[4 - i] = odd - even
    out[2] = float(D[2, 0]) * d0 + float(D[2, 1]) * d1
    return out


def backward(h):
    s0, s1, d0, d1 = h[0] + h[4], h[1] + h[3], h[0] - h[4], h[1] - h[3]
    out = [None] * 5
    for p in range(2):
        even = (
            float((D[0, p] + D[4, p]) / 2) * s0
            + float((D[1, p] + D[3, p]) / 2) * s1
            + float(D[2, p]) * h[2]
        )
        odd = float((D[0, p] - D[4, p]) / 2) * d0 + float((D[1, p] - D[3, p]) / 2) * d1
        out[p] = even + odd
        out[4 - p] = odd - even
    out[2] = float(D[0, 2]) * d0 + float(D[1, 2]) * d1
    return out


def body(
    n_surf,
    n_depth,
    wave_ref,
    adj_ref,
    density_ref,
    modulus_ref,
    cell_ref,
    elem_ref,
    brick_ref,
    count_ref,
    spread_ref,
    fold_ref,
    expand_ref,
    gather_ref,
    select_ref,
    scale_ref,
    force_ref,
    mass_ref,
    blocks_ref,
    fields,
    halo_a,
    halo_c,
    halo_d,
    stage_a,
    stage_c,
    lhs,
    values,
    stiff,
    product,
    forces,
    folded,
    mass_lhs,
    mass_fold,
    mass_sum,
    face_a,
    face_c,
    face_d,
    got_a,
    got_c,
    got_d,
    own_block,
    got_blocks,
    load_sem,
    send_sem,
    recv_sem,
):
    s = lax.axis_index("surf")
    d = lax.axis_index("depth")
    above_s, above_d = s < n_surf - 1, d < n_depth - 1
    below_s, below_d = s > 0, d > 0
    above_both, below_both = above_s & above_d, below_s & below_d
    up = ((s + 1, d, above_s), (s, d + 1, above_d), (s + 1, d + 1, above_both))
    down = ((s - 1, d, below_s), (s, d - 1, below_d), (s - 1, d - 1, below_both))

    loads = [
        pltpu.make_async_copy(wave_ref, fields.at[pl.ds(0, 4 * PLANE)], load_sem.at[0]),
        pltpu.make_async_copy(adj_ref, fields.at[pl.ds(4 * PLANE, 4 * PLANE)], load_sem.at[1]),
    ]
    for load in loads:
        load.start()
    barrier = pltpu.get_barrier_semaphore()
    for to_s, to_d, there in up + down:

        @pl.when(there)
        def _():
            pl.semaphore_signal(barrier, inc=1, device_id=(to_s, to_d), device_id_type=MESH)

    for load in loads:
        load.wait()
    for c in range(NODES_C):
        stage_a[c * 8 : c * 8 + 8, :] = fields[pl.ds(c, 8, stride=PLANE), :]
    for a in range(NODES_A):
        stage_c[a * 8 : a * 8 + 8, :] = fields[pl.ds(a * NODES_C, 8, stride=PLANE), :]
    peers = sum(there.astype(jnp.int32) for _, _, there in up + down)
    pl.semaphore_wait(barrier, peers)

    def remote(source, target, k, to):
        return pltpu.make_async_remote_copy(
            src_ref=source,
            dst_ref=target,
            send_sem=send_sem.at[k],
            recv_sem=recv_sem.at[k],
            device_id=(to[0], to[1]),
            device_id_type=MESH,
        )

    halos = [
        remote(stage_a, halo_a, 0, down[0]),
        remote(stage_c, halo_c, 1, down[1]),
        remote(stage_a.at[pl.ds(0, 8)], halo_d, 2, down[2]),
    ]
    for copy, (_, _, there) in zip(halos, down):

        @pl.when(there)
        def _():
            copy.start()

    rows = lax.broadcasted_iota(jnp.int32, (256, 256), 0)
    placing = jnp.where(cell_ref[0:1, :] == rows, 1.0, 0.0).astype(bf16)

    def to_cells(ref):
        high, low = two_terms(ref[...])
        return dot_rows(high, placing) + dot_rows(low, placing)

    scale = jnp.concatenate([scale_ref[0:125, :]] * 2, axis=1)
    density = to_cells(density_ref) * scale
    modulus = to_cells(modulus_ref) * scale
    pad = jnp.zeros((3, 256), f32)
    density = jnp.concatenate([density, pad], axis=0)
    modulus = jnp.concatenate([modulus, pad], axis=0)
    stiff[...] = dot_right(expand_ref[...], density)
    picked = dot_right(select_ref[...], modulus)
    for r in range(5):
        mass_lhs[:, r * 128 : (r + 1) * 128] = (
            picked[r * 96 : r * 96 + 48, 0:128] + picked[r * 96 + 48 : r * 96 + 96, 128:256]
        )
    mass_fold[...] = dot_left(mass_lhs[...], fold_ref[...])
    for a in range(NODES_A + 1):
        for ec in range(4):
            lanes = slice(ec * 128, ec * 128 + 128)
            mass_sum[a * 24 + 4 * ec : a * 24 + 4 * ec + 4, :] = mass_fold[a * 5 : a * 5 + 4, lanes]
        for ec in range(4):
            lanes = slice(ec * 128, ec * 128 + 128)
            tail = mass_fold[a * 5 + 4 : a * 5 + 5, lanes]
            row = a * 24 + 4 * ec + 4
            if ec < 3:
                mass_sum[row : row + 1, :] += tail
            else:
                mass_sum[row : row + 1, :] = tail

    slots = lax.broadcasted_iota(jnp.int32, (1, 256), 1)
    digit_rows = lax.broadcasted_iota(jnp.int32, (16, 256), 0)
    digits = jnp.zeros((16, 256), f32)
    for t in range(4):
        live = slots < count_ref[0, t]
        number = jnp.where(live, brick_ref[t : t + 1, :] + 1, 0)
        pair = jnp.where(
            digit_rows == 2 * t,
            number >> 5,
            jnp.where(digit_rows == 2 * t + 1, number & 31, 0),
        )
        listed = jnp.where(elem_ref[t : t + 1, :] == rows, 1.0, 0.0).astype(bf16)
        digits = digits + dot_rows(pair.astype(f32).astype(bf16), listed)
    own_block[128:144, :] = dot_rows(digits.astype(bf16), placing)

    zeros = jnp.zeros((8, 128), f32)
    lhs[360:384, :] = jnp.zeros((24, 512), f32)

    def place(a, c, tile):
        ec, q = c // 4, c % 4
        if ec < 4:
            lhs[pl.ds(pl.multiple_of((a * 5 + q) * 8, 8), 8), ec * 128 : ec * 128 + 128] = tile
        if q == 0 and ec > 0:
            lhs[pl.ds(pl.multiple_of((a * 5 + 4) * 8, 8), 8), (ec - 1) * 128 : ec * 128] = tile

    def place_plane(a, carry):
        for c in range(NODES_C):
            place(a, c, fields[pl.ds(a * NODES_C + c, 8, stride=PLANE), :])
        return carry

    lax.fori_loop(0, NODES_A, place_plane, 0)

    for buffer, (_, _, there) in zip((halo_a, halo_c, halo_d), up):

        @pl.when(jnp.logical_not(there))
        def _():
            buffer[...] = jnp.zeros(buffer.shape, f32)

    for copy, (_, _, there) in zip(halos, down):

        @pl.when(there)
        def _():
            copy.wait_send()

    for copy, (_, _, there) in zip(halos, up):

        @pl.when(there)
        def _():
            copy.wait_recv()

    for c in range(NODES_C):
        place(8, c, halo_a[c * 8 : c * 8 + 8, :])
    for a in range(NODES_A):
        place(a, 16, halo_c[a * 8 : a * 8 + 8, :])
    place(8, 16, halo_d[...])

    def spread_rows(k, carry):
        at = pl.ds(pl.multiple_of(k * 128, 128), 128)
        values[at, :] = dot_left(lhs[at, :], spread_ref[...])
        return carry

    lax.fori_loop(0, 3, spread_rows, 0)
    product[1000:1024, :] = jnp.zeros((24, 256), f32)

    def mates(g):
        return g * pltpu.roll(g, 4, 0)

    def eight(k):
        return pl.ds(pl.multiple_of(k * 8, 8), 8)

    for ea in range(2):
        half = slice(ea * 128, ea * 128 + 128)

        def plane(p, carry):
            v = [
                [
                    values[eight((4 * ea + p) * 5 + q), r * 128 : r * 128 + 128]
                    for r in range(5)
                ]
                for q in range(5)
            ]
            k = [[stiff[eight(p * 25 + q * 5 + r), half] for r in range(5)] for q in range(5)]
            pair = [[None] * 5 for _ in range(5)]
            force = [[None] * 5 for _ in range(5)]
            for r in range(5):
                g = forward([v[q][r] for q in range(5)])
                f = backward([k[q][r] * g[q] for q in range(5)])
                for q in range(5):
                    pair[q][r] = mates(g[q])
                    force[q][r] = f[q]
            for q in range(5):
                g = forward(v[q])
                f = backward([k[q][r] * g[r] for r in range(5)])
                for r in range(5):
                    product[eight(p * 25 + q * 5 + r), half] = pair[q][r] + mates(g[r])
                    forces[eight(ea * 25 + p * 5 + q), r * 128 : r * 128 + 128] = force[q][r] + f[r]
            return carry

        lax.fori_loop(0, 5, plane, 0)

        def line(q, carry):
            for r in range(5):
                lanes = slice(r * 128, r * 128 + 128)
                g = forward([values[eight((4 * ea + p) * 5 + q), lanes] for p in range(5)])
                f = backward([stiff[eight(p * 25 + q * 5 + r), half] * g[p] for p in range(5)])
                for p in range(5):
                    product[eight(p * 25 + q * 5 + r), half] += mates(g[p])
                    forces[eight(ea * 25 + p * 5 + q), lanes] += f[p]
            return carry

        lax.fori_loop(0, 5, line, 0)

    own_block[0:128, :] = dot_right(gather_ref[...], product[...]) * (
        -time_step * jnp.concatenate([scale_ref[...]] * 2, axis=1)
    )
    sends = [remote(own_block, got_blocks.at[k], 3 + k, up[k]) for k in range(3)]
    for copy, (_, _, there) in zip(sends, up):

        @pl.when(there)
        def _():
            copy.start()

    for k in range(3):

        @pl.when(jnp.logical_not(down[k][2]))
        def _():
            got_blocks[k] = jnp.zeros((BLOCK_ROWS, 256), f32)

    forces[160:200, :] += forces[200:240, :]

    def fold_rows(first, count, at):
        folded[at : at + count, :] = dot_left(forces[first : first + count, :], fold_ref[...])

    fold_rows(0, 200, 0)
    fold_rows(240, 160, 200)

    def node(a, c):
        ec, q = c // 4, c % 4
        out = None
        if ec < 4:
            out = folded[eight(a * 5 + q), ec * 128 : ec * 128 + 128]
        if q == 0 and ec > 0:
            tail = folded[eight(a * 5 + 4), (ec - 1) * 128 : ec * 128]
            out = tail if out is None else out + tail
        return out

    for c in range(NODES_C):
        face_a[c * 8 : c * 8 + 8, :] = node(8, c)
    face_a[128:144, :] = mass_sum[192:208, :]
    for a in range(NODES_A):
        face_c[a * 8 : a * 8 + 8, :] = node(a, 16)
        face_c[64 + a : 65 + a, :] = mass_sum[a * 24 + 16 : a * 24 + 17, :]
    face_d[0:8, :] = node(8, 16)
    face_d[8:16, :] = jnp.broadcast_to(mass_sum[208:209, :], (8, 128))
    faces = [
        remote(face_a, got_a, 6, up[0]),
        remote(face_c, got_c, 7, up[1]),
        remote(face_d, got_d, 8, up[2]),
    ]
    for copy, (_, _, there) in zip(faces, up):

        @pl.when(there)
        def _():
            copy.start()

    for buffer, (_, _, there) in zip((got_a, got_c, got_d), down):

        @pl.when(jnp.logical_not(there))
        def _():
            buffer[...] = jnp.zeros(buffer.shape, f32)

    def write_plane(a, carry):
        for c in range(1, NODES_C):
            force_ref[pl.ds(a * NODES_C + c, 8, stride=PLANE), :] = node(a, c)
        return carry

    lax.fori_loop(1, NODES_A, write_plane, 0)

    for copy, (_, _, there) in zip(faces, up):

        @pl.when(there)
        def _():
            copy.wait_send()

    for copy, (_, _, there) in zip(faces, down):

        @pl.when(there)
        def _():
            copy.wait_recv()

    for c in range(1, NODES_C):
        force_ref[pl.ds(c, 8, stride=PLANE), :] = node(0, c) + got_a[c * 8 : c * 8 + 8, :]
    for a in range(1, NODES_A):
        force_ref[pl.ds(a * NODES_C, 8, stride=PLANE), :] = (
            node(a, 0) + got_c[a * 8 : a * 8 + 8, :]
        )
    force_ref[pl.ds(0, 8, stride=PLANE), :] = (
        node(0, 0) + got_a[0:8, :] + got_c[0:8, :] + got_d[0:8, :]
    )
    mass_sum[0:16, :] += got_a[128:144, :]
    for a in range(NODES_A):
        mass_sum[a * 24 : a * 24 + 1, :] += got_c[64 + a : 65 + a, :]
    mass_sum[0:1, :] += got_d[8:9, :]
    for a in range(NODES_A):
        mass_ref[a * 16 : a * 16 + 16, :] = mass_sum[a * 24 : a * 24 + 16, :]

    for copy, (_, _, there) in zip(sends, up):

        @pl.when(there)
        def _():
            copy.wait_send()

    blocks_ref[0] = own_block[...]
    for k, (copy, (_, _, there)) in enumerate(zip(sends, down)):

        @pl.when(there)
        def _():
            copy.wait_recv()

        blocks_ref[1 + k] = got_blocks[k]


def per_device(
    n_surf,
    n_depth,
    wave_now,
    wave_old,
    adj_now,
    adj_old,
    source,
    adj_source,
    inv_density,
    inv_modulus,
    element_cell,
    send_elem,
    send_brick,
    send_count,
):
    constants, scale = tables()
    vmem = pl.BlockSpec(memory_space=pltpu.VMEM)
    anywhere = pl.BlockSpec(memory_space=pl.ANY)
    smem = pl.BlockSpec(memory_space=pltpu.SMEM)
    force, mass, blocks = pl.pallas_call(
        functools.partial(body, n_surf, n_depth),
        out_shape=(
            jax.ShapeDtypeStruct((8 * PLANE, 128), f32),
            jax.ShapeDtypeStruct((PLANE, 128), f32),
            jax.ShapeDtypeStruct((4, BLOCK_ROWS, 256), f32),
        ),
        in_specs=[anywhere] * 2 + [vmem] * 5 + [smem] + [vmem] * 6,
        out_specs=(vmem,) * 3,
        scratch_shapes=[
            pltpu.VMEM((8 * PLANE, 128), f32),
            pltpu.VMEM((128, 128), f32),
            pltpu.VMEM((64, 128), f32),
            pltpu.VMEM((8, 128), f32),
            pltpu.VMEM((128, 128), f32),
            pltpu.VMEM((64, 128), f32),
            pltpu.VMEM((384, 512), f32),
            pltpu.VMEM((384, 640), f32),
            pltpu.VMEM((1000, 256), f32),
            pltpu.VMEM((1024, 256), f32),
            pltpu.VMEM((400, 640), f32),
            pltpu.VMEM((360, 512), f32),
            pltpu.VMEM((48, 640), f32),
            pltpu.VMEM((48, 512), f32),
            pltpu.VMEM((216, 128), f32),
            pltpu.VMEM((FACE_A, 128), f32),
            pltpu.VMEM((FACE_C, 128), f32),
            pltpu.VMEM((FACE_D, 128), f32),
            pltpu.VMEM((FACE_A, 128), f32),
            pltpu.VMEM((FACE_C, 128), f32),
            pltpu.VMEM((FACE_D, 128), f32),
            pltpu.VMEM((BLOCK_ROWS, 256), f32),
            pltpu.VMEM((3, BLOCK_ROWS, 256), f32),
            pltpu.SemaphoreType.DMA((2,)),
            pltpu.SemaphoreType.DMA((9,)),
            pltpu.SemaphoreType.DMA((9,)),
        ],
        compiler_params=pltpu.CompilerParams(
            collective_id=0, has_side_effects=True, vmem_limit_bytes=40 * 1024 * 1024
        ),
    )(
        wave_now.reshape(4 * PLANE, 128),
        adj_now.reshape(4 * PLANE, 128),
        inv_density,
        inv_modulus,
        element_cell,
        send_elem[0],
        send_brick[0],
        send_count,
        *[jnp.asarray(c, bf16) for c in constants],
        jnp.asarray(scale, f32),
    )
    force = force.reshape(8, NODES_A, NODES_C, 128)
    mass = mass.reshape(1, NODES_A, NODES_C, 128)
    step_square = time_step * time_step
    wave_next = 2.0 * wave_now - wave_old + step_square * (source - force[:4]) / mass
    adj_next = 2.0 * adj_now - adj_old + step_square * (adj_source - force[4:]) / mass
    brick_dev = 1024
    brick_ids = jnp.arange(brick_dev, dtype=jnp.int32).astype(f32)
    brick_kernel = 0.0
    for t in range(4):
        targets = blocks[t, 128 + 2 * t] * 32.0 + blocks[t, 129 + 2 * t] - 1.0
        selector = (targets[:, None] == brick_ids[None, :]).astype(f32)
        brick_kernel = brick_kernel + jnp.dot(
            blocks[t, :125], selector, precision=precise, preferred_element_type=f32
        )
    return wave_next, adj_next, brick_kernel


def solution(mesh):
    field = P(None, "surf", "depth", None)
    column = P(None, ("surf", "depth"))
    placed = (field,) * 6 + (
        column,
        column,
        P(("surf", "depth"), None),
        P(("surf", "depth"), None, None),
        P(("surf", "depth"), None, None),
        P(("surf", "depth"), None),
    )
    return jax.shard_map(
        functools.partial(per_device, mesh.shape["surf"], mesh.shape["depth"]),
        mesh=mesh,
        in_specs=placed,
        out_specs=(field, field, column),
        check_vma=False,
    )
```

profile of v0, /device:TPU:9, one launch (start us, length us, event | category | flops | bytes accessed | tf_op | source)
XLA Modules:
  0.0 38.2 jit_solution(8488867577341276484)
XLA Ops:
  0.6 0.0 copy-start.10
  0.6 0.0 copy-start.12
  0.7 0.0 copy-start.13
  0.7 0.7 %copy-done.10 = s32[1,4,256]{2,1,0:T(4,128)S(1)} copy-done((s32[1,4,256]{2,1,0:T(4,128)S(1)}, s32[1,4,256]{2,1,0:T(4,128)}, u32[]{:S(2)}) %copy-start.10) | copy-done | bytes 4120
  1.3 0.0 copy-done.12
  1.3 0.0 copy-done.13
  1.3 0.0 copy-start
  1.3 0.9 %copy-done = f32[4,8,16,128]{3,2,1,0:T(8,128)S(1)} copy-done((f32[4,8,16,128]{3,2,1,0:T(8,128)S(1)}, f32[4,8,16,128]{3,2,1,0:T(8,128)}, u32[]{:S(2)}) %copy-start) | copy-done | bytes 262168
  2.3 0.0 copy-start.1
  2.3 0.9 %copy-done.1 = f32[4,8,16,128]{3,2,1,0:T(8,128)S(1)} copy-done((f32[4,8,16,128]{3,2,1,0:T(8,128)S(1)}, f32[4,8,16,128]{3,2,1,0:T(8,128)}, u32[]{:S(2)}) %copy-start.1) | copy-done | bytes 262168
  3.2 0.0 copy-start.2
  3.2 1.1 %copy-done.2 = bf16[512,640]{1,0:T(8,128)(2,1)S(1)} copy-done((bf16[512,640]{1,0:T(8,128)(2,1)S(1)}, bf16[512,640]{1,0:T(8,128)(2,1)}, u32[]{:S(2)}) %copy-start.2) | copy-done | bytes 655384
  4.3 0.0 copy-start.3
  4.3 1.1 %copy-done.3 = bf16[640,512]{1,0:T(8,128)(2,1)S(1)} copy-done((bf16[640,512]{1,0:T(8,128)(2,1)S(1)}, bf16[640,512]{1,0:T(8,128)(2,1)}, u32[]{:S(2)}) %copy-start.3) | copy-done | bytes 655384
  5.4 0.0 copy-start.4
  5.4 0.9 %copy-done.4 = bf16[128,1024]{1,0:T(8,128)(2,1)S(1)} copy-done((bf16[128,1024]{1,0:T(8,128)(2,1)S(1)}, bf16[128,1024]{1,0:T(8,128)(2,1)}, u32[]{:S(2)}) %copy-start.4) | copy-done | bytes 262168
  6.4 0.0 copy-start.5
  6.4 0.9 %copy-done.5 = bf16[1000,128]{1,0:T(8,128)(2,1)S(1)} copy-done((bf16[1000,128]{1,0:T(8,128)(2,1)S(1)}, bf16[1000,128]{1,0:T(8,128)(2,1)}, u32[]{:S(2)}) %copy-start.5) | copy-done | bytes 256024
  7.3 0.0 copy-start.6
  7.3 0.9 %copy-done.6 = f32[125,256]{1,0:T(8,128)S(1)} copy-done((f32[125,256]{1,0:T(8,128)S(1)}, f32[125,256]{1,0:T(8,128)}, u32[]{:S(2)}) %copy-start.6) | copy-done | bytes 128024
  8.2 0.0 copy-start.7
  8.2 0.9 %copy-done.7 = f32[125,256]{1,0:T(8,128)S(1)} copy-done((f32[125,256]{1,0:T(8,128)S(1)}, f32[125,256]{1,0:T(8,128)}, u32[]{:S(2)}) %copy-start.7) | copy-done | bytes 128024
  9.1 0.0 copy-start.8
  9.1 0.9 %copy-done.8 = bf16[480,128]{1,0:T(8,128)(2,1)S(1)} copy-done((bf16[480,128]{1,0:T(8,128)(2,1)S(1)}, bf16[480,128]{1,0:T(8,128)(2,1)}, u32[]{:S(2)}) %copy-start.8) | copy-done | bytes 122904
  10.0 0.0 copy-start.9
  10.0 0.8 %copy-done.9 = f32[128,128]{1,0:T(8,128)S(1)} copy-done((f32[128,128]{1,0:T(8,128)S(1)}, f32[128,128]{1,0:T(8,128)}, u32[]{:S(2)}) %copy-start.9) | copy-done | bytes 65560
  10.9 0.0 copy-start.11
  10.9 0.7 %copy-done.11 = s32[1,4,256]{2,1,0:T(4,128)S(1)} copy-done((s32[1,4,256]{2,1,0:T(4,128)S(1)}, s32[1,4,256]{2,1,0:T(4,128)}, u32[]{:S(2)}) %copy-start.11) | copy-done | bytes 4120
  11.5 21.6 %shard_map.193 = (f32[1024,128]{1,0:T(8,128)S(1)}, f32[128,128]{1,0:T(8,128)S(1)}, f32[4,144,256]{2,1,0:T(8,128)S(1)}) custom-call(f32[512,128]{1,0:T(8,128)S(1)} %bitcast.23, f32[512,128]{1,0:T(8,128)S(1)} %bitcast.24, f32[125,256]{1,0:T(8,128)S(1)} %copy-done.6, f32[125,256]{1,0:T(8,128)S(1)} %copy-done.7, s32[1,256]{1,0:T(1,128)S(1)} %copy-done.12, ...), custom_call_target="tpu_custom_call" | custom-call | tf_op jit(solution)/shard_map/pallas_call | solution.py:490
  33.1 0.0 copy-start.14
  33.1 0.0 copy-start.15
  33.1 0.0 copy-start.16
  33.1 0.0 copy-start.17
  33.2 0.9 %copy-done.14 = f32[4,8,16,128]{3,2,1,0:T(8,128)S(1)} copy-done((f32[4,8,16,128]{3,2,1,0:T(8,128)S(1)}, f32[4,8,16,128]{3,2,1,0:T(8,128)}, u32[]{:S(2)}) %copy-start.14) | copy-done | bytes 262168
  34.1 0.1 copy-done.15
  34.1 0.1 copy-done.16
  34.2 0.1 copy-done.17
  34.3 0.9 %divide_add_fusion = (f32[4,8,16,128]{3,2,1,0:T(8,128)}, f32[4,8,16,128]{3,2,1,0:T(8,128)}) fusion(f32[4,8,16,128]{3,2,1,0:T(8,128)S(1)} %copy-done.14, f32[4,8,16,128]{3,2,1,0:T(8,128)S(1)} %bitcast.28, f32[4,8,16,128]{3,2,1,0:T(8,128)S(1)} %copy-done.15, f32[4,8,16,128]{3,2,1,0:T(8,128)S(1)} %copy-done.1, f32[8,16,128]{2,1,0:T(8,128)S(1)} %bitcast.25, ...), kind=kLoop, calls=%fused_computation.16 | loop fusion | flops 786432 | bytes 2686976 | tf_op jit(solution)/shard_map/add | solution.py:546
  35.3 0.5 %fusion.3 = f32[125,1024]{1,0:T(8,128)S(1)} fusion(f32[1024]{0:T(1024)S(1)} %iota_convert_fusion, f32[256]{0:T(256)S(1)} %bitcast.30, f32[4,144,256]{2,1,0:T(8,128)S(1)} %get-tuple-element.8), kind=kOutput, calls=%fused_computation.6 | convolution fusion | flops 393478144 | bytes 648192 | tf_op jit(solution)/shard_map/dot_general | solution.py:553
  35.8 0.5 %convolution_add_fusion.2 = f32[125,1024]{1,0:T(8,128)S(1)} fusion(f32[125,1024]{1,0:T(8,128)S(1)} %fusion.3, f32[1024]{0:T(1024)S(1)} %iota_convert_fusion, f32[256]{0:T(256)S(1)} %bitcast.33, f32[4,144,256]{2,1,0:T(8,128)S(1)} %get-tuple-element.8), kind=kOutput, calls=%fused_computation.2 | convolution fusion | flops 393606144 | bytes 1172480 | tf_op jit(solution)/shard_map/dot_general | solution.py:553
  36.3 0.5 %convolution_add_fusion.1 = f32[125,1024]{1,0:T(8,128)S(1)} fusion(f32[125,1024]{1,0:T(8,128)S(1)} %convolution_add_fusion.2, f32[1024]{0:T(1024)S(1)} %iota_convert_fusion, f32[256]{0:T(256)S(1)} %bitcast.32, f32[4,144,256]{2,1,0:T(8,128)S(1)} %get-tuple-element.8), kind=kOutput, calls=%fused_computation.1 | convolution fusion | flops 393606144 | bytes 1172480 | tf_op jit(solution)/shard_map/dot_general | solution.py:553
  36.9 1.3 %convolution_add_fusion = f32[125,1024]{1,0:T(8,128)} fusion(f32[125,1024]{1,0:T(8,128)S(1)} %convolution_add_fusion.1, f32[1024]{0:T(1024)S(1)} %iota_convert_fusion, f32[256]{0:T(256)S(1)} %bitcast.31, f32[4,144,256]{2,1,0:T(8,128)S(1)} %get-tuple-element.8), kind=kOutput, calls=%fused_computation | convolution fusion | flops 393606144 | bytes 1172480 | tf_op jit(solution)/shard_map/dot_general | solution.py:553
  (3 shorter events, 0.1 us)
Async XLA Ops:
  0.6 0.7 %copy-start.10 = (s32[1,4,256]{2,1,0:T(4,128)S(1)}, s32[1,4,256]{2,1,0:T(4,128)}, u32[]{:S(2)}) copy-start(s32[1,4,256]{2,1,0:T(4,128)} %param.27) | copy-start | bytes 12292
  0.6 0.7 %copy-start.12 = (s32[1,256]{1,0:T(1,128)S(1)}, s32[1,256]{1,0:T(1,128)}, u32[]{:S(2)}) copy-start(s32[1,256]{1,0:T(1,128)} %cell_ref.1) | copy-start | bytes 3076
  0.7 0.7 %copy-start.13 = (s32[1,4]{1,0:T(1,128)S(1)}, s32[1,4]{1,0:T(1,128)}, u32[]{:S(2)}) copy-start(s32[1,4]{1,0:T(1,128)} %count_ref.1) | copy-start | bytes 52
  1.3 1.0 %copy-start = (f32[4,8,16,128]{3,2,1,0:T(8,128)S(1)}, f32[4,8,16,128]{3,2,1,0:T(8,128)}, u32[]{:S(2)}) copy-start(f32[4,8,16,128]{3,2,1,0:T(8,128)} %param.18) | copy-start | bytes 786436
  2.3 0.9 %copy-start.1 = (f32[4,8,16,128]{3,2,1,0:T(8,128)S(1)}, f32[4,8,16,128]{3,2,1,0:T(8,128)}, u32[]{:S(2)}) copy-start(f32[4,8,16,128]{3,2,1,0:T(8,128)} %param.20) | copy-start | bytes 786436
  3.2 1.1 %copy-start.2 = (bf16[512,640]{1,0:T(8,128)(2,1)S(1)}, bf16[512,640]{1,0:T(8,128)(2,1)}, u32[]{:S(2)}) copy-start(bf16[512,640]{1,0:T(8,128)(2,1)} %constant.24.clone.spread_ref) | copy-start | bytes 1966084
  4.3 1.1 %copy-start.3 = (bf16[640,512]{1,0:T(8,128)(2,1)S(1)}, bf16[640,512]{1,0:T(8,128)(2,1)}, u32[]{:S(2)}) copy-start(bf16[640,512]{1,0:T(8,128)(2,1)} %constant.25.clone.fold_ref) | copy-start | bytes 1966084
  5.4 0.9 %copy-start.4 = (bf16[128,1024]{1,0:T(8,128)(2,1)S(1)}, bf16[128,1024]{1,0:T(8,128)(2,1)}, u32[]{:S(2)}) copy-start(bf16[128,1024]{1,0:T(8,128)(2,1)} %constant.27.clone.gather_ref) | copy-start | bytes 786436
  6.4 0.9 %copy-start.5 = (bf16[1000,128]{1,0:T(8,128)(2,1)S(1)}, bf16[1000,128]{1,0:T(8,128)(2,1)}, u32[]{:S(2)}) copy-start(bf16[1000,128]{1,0:T(8,128)(2,1)} %constant.26.clone.expand_ref) | copy-start | bytes 768004
  7.3 0.9 %copy-start.6 = (f32[125,256]{1,0:T(8,128)S(1)}, f32[125,256]{1,0:T(8,128)}, u32[]{:S(2)}) copy-start(f32[125,256]{1,0:T(8,128)} %density_ref.1) | copy-start | bytes 384004
  8.2 0.9 %copy-start.7 = (f32[125,256]{1,0:T(8,128)S(1)}, f32[125,256]{1,0:T(8,128)}, u32[]{:S(2)}) copy-start(f32[125,256]{1,0:T(8,128)} %modulus_ref.1) | copy-start | bytes 384004
  9.1 0.9 %copy-start.8 = (bf16[480,128]{1,0:T(8,128)(2,1)S(1)}, bf16[480,128]{1,0:T(8,128)(2,1)}, u32[]{:S(2)}) copy-start(bf16[480,128]{1,0:T(8,128)(2,1)} %constant.28.clone.select_ref) | copy-start | bytes 368644
  10.0 0.8 %copy-start.9 = (f32[128,128]{1,0:T(8,128)S(1)}, f32[128,128]{1,0:T(8,128)}, u32[]{:S(2)}) copy-start(f32[128,128]{1,0:T(8,128)} %constant.29.clone.scale_ref) | copy-start | bytes 196612
  10.9 0.7 %copy-start.11 = (s32[1,4,256]{2,1,0:T(4,128)S(1)}, s32[1,4,256]{2,1,0:T(4,128)}, u32[]{:S(2)}) copy-start(s32[1,4,256]{2,1,0:T(4,128)} %param.28) | copy-start | bytes 12292
  33.1 1.0 %copy-start.14 = (f32[4,8,16,128]{3,2,1,0:T(8,128)S(1)}, f32[4,8,16,128]{3,2,1,0:T(8,128)}, u32[]{:S(2)}) copy-start(f32[4,8,16,128]{3,2,1,0:T(8,128)} %param.23) | copy-start | bytes 786436
  33.1 1.0 %copy-start.15 = (f32[4,8,16,128]{3,2,1,0:T(8,128)S(1)}, f32[4,8,16,128]{3,2,1,0:T(8,128)}, u32[]{:S(2)}) copy-start(f32[4,8,16,128]{3,2,1,0:T(8,128)} %param.21) | copy-start | bytes 786436
  33.1 1.1 %copy-start.16 = (f32[4,8,16,128]{3,2,1,0:T(8,128)S(1)}, f32[4,8,16,128]{3,2,1,0:T(8,128)}, u32[]{:S(2)}) copy-start(f32[4,8,16,128]{3,2,1,0:T(8,128)} %param.22) | copy-start | bytes 786436
  33.1 1.2 %copy-start.17 = (f32[4,8,16,128]{3,2,1,0:T(8,128)S(1)}, f32[4,8,16,128]{3,2,1,0:T(8,128)}, u32[]{:S(2)}) copy-start(f32[4,8,16,128]{3,2,1,0:T(8,128)} %param.19) | copy-start | bytes 786436
where the time goes:
time: 38.7 us; the launch traced here: 38.2 us
  Pallas kernels  21.6 us (56%)
  local copies, waits for them, and re-layouts  12 us (31%)
  matrix products  2.93 us (8%)
  other arithmetic  0.95 us (2%)
  between operations  0.75 us (2%)
    pallas_call x1, Pallas kernels, per_device(): pl.pallas_call(functools.partial(body, n_surf, n_depth), out_shape=(jax.S...  21.6 us
    unnamed x36, local copies, waits for them, and re-layouts  12 us
    dot_general x4, matrix products, per_device(): jnp.dot(blocks[t, :125], selector, precision=precise, preferred_element_t...  2.93 us
    add x1, other arithmetic, per_device(): 2.0 * adj_now - adj_old + step_square * (adj_source - force[4:]) / mass  0.93 us

commit v1 on v0

--- a/solution.py
+++ b/solution.py
@@ -10,7 +10,6 @@
 from jax.sharding import PartitionSpec as P
 
 time_step = 0.05
-precise = lax.Precision.HIGHEST
 MESH = pl.DeviceIdType.MESH
 f32 = jnp.float32
 bf16 = jnp.bfloat16
@@ -37,26 +36,30 @@
 D, W = gll_numbers()
 
 
-def tables():
-    spread = np.zeros((512, 640), np.float32)
-    for ec in range(4):
-        for eb in range(32):
-            for r in range(5):
-                spread[ec * 128 + (4 * eb + r) % 128, r * 128 + ec * 32 + eb] = 1.0
-    expand = np.zeros((1000, 128), np.float32)
-    expand[np.arange(1000), np.arange(1000) // 8] = 1.0
-    gather = np.zeros((128, 1024), np.float32)
-    gather[np.arange(1000) // 8, np.arange(1000)] = 0.5
-    select = np.zeros((480, 128), np.float32)
-    for r in range(5):
-        for ea in range(2):
-            for p in range(5):
-                for q in range(5):
-                    select[(r * 2 + ea) * 48 + (4 * ea + p) * 5 + q, p * 25 + q * 5 + r] = 1.0
+def cubature_rows():
     cubature = (W[:, None, None] * W[None, :, None] * W[None, None, :]).reshape(-1)
     scale = np.zeros((128, 128), np.float32)
     scale[:125] = cubature[:, None]
-    return (spread, spread.T.copy(), expand, gather, select), scale
+    return scale
+
+
+def iota(shape, axis):
+    return lax.broadcasted_iota(jnp.int32, shape, axis)
+
+
+def ones_where(condition, one=1.0):
+    return jnp.where(condition, one, 0.0).astype(bf16)
+
+
+def fill_tables(spread_ref, fold_ref):
+    row, lane = iota((128, 128), 0), iota((128, 128), 1)
+    lane_one, row_one = iota((1, 128), 1), iota((128, 1), 0)
+    for ec in range(4):
+        for r in range(5):
+            node = jnp.where(lane_one >> 5 == ec, (4 * (lane_one & 31) + r) & 127, -1)
+            spread_ref[ec * 128 : ec * 128 + 128, r * 128 : r * 128 + 128] = ones_where(row == node)
+            node = jnp.where(row_one >> 5 == ec, (4 * (row_one & 31) + r) & 127, -1)
+            fold_ref[r * 128 : r * 128 + 128, ec * 128 : ec * 128 + 128] = ones_where(lane == node)
 
 
 def two_terms(x):
@@ -117,24 +120,37 @@
 def body(
     n_surf,
     n_depth,
-    wave_ref,
-    adj_ref,
-    density_ref,
-    modulus_ref,
+    wave_hbm,
+    adj_hbm,
+    cell_hbm,
+    elem_hbm,
+    brick_hbm,
+    count_hbm,
+    density_hbm,
+    modulus_hbm,
+    scale_hbm,
+    wave_old_hbm,
+    adj_old_hbm,
+    source_hbm,
+    adj_source_hbm,
+    wave_out,
+    adj_out,
+    brick_out,
+    next_ref,
+    blocks_ref,
+    bricks,
+    fields,
     cell_ref,
     elem_ref,
     brick_ref,
     count_ref,
+    density_ref,
+    modulus_ref,
+    scale_ref,
+    fold_ref,
     spread_ref,
-    fold_ref,
-    expand_ref,
-    gather_ref,
-    select_ref,
-    scale_ref,
-    force_ref,
-    mass_ref,
-    blocks_ref,
-    fields,
+    old,
+    driven,
     halo_a,
     halo_c,
     halo_d,
@@ -155,8 +171,7 @@
     got_a,
     got_c,
     got_d,
-    own_block,
-    got_blocks,
+    write_sem,
     load_sem,
     send_sem,
     recv_sem,
@@ -169,9 +184,25 @@
     up = ((s + 1, d, above_s), (s, d + 1, above_d), (s + 1, d + 1, above_both))
     down = ((s - 1, d, below_s), (s, d - 1, below_d), (s - 1, d - 1, below_both))
 
+    first, second = pl.ds(0, 4 * PLANE), pl.ds(4 * PLANE, 4 * PLANE)
+    moves = [
+        (wave_hbm, fields.at[first]),
+        (adj_hbm, fields.at[second]),
+        (cell_hbm, cell_ref),
+        (density_hbm, density_ref),
+        (modulus_hbm, modulus_ref),
+        (scale_hbm, scale_ref),
+        (elem_hbm, elem_ref),
+        (brick_hbm, brick_ref),
+        (count_hbm, count_ref),
+        (wave_old_hbm, old.at[first]),
+        (adj_old_hbm, old.at[second]),
+        (source_hbm, driven.at[first]),
+        (adj_source_hbm, driven.at[second]),
+    ]
     loads = [
-        pltpu.make_async_copy(wave_ref, fields.at[pl.ds(0, 4 * PLANE)], load_sem.at[0]),
-        pltpu.make_async_copy(adj_ref, fields.at[pl.ds(4 * PLANE, 4 * PLANE)], load_sem.at[1]),
+        pltpu.make_async_copy(source, target, load_sem.at[k])
+        for k, (source, target) in enumerate(moves)
     ]
     for load in loads:
         load.start()
@@ -182,7 +213,8 @@
         def _():
             pl.semaphore_signal(barrier, inc=1, device_id=(to_s, to_d), device_id_type=MESH)
 
-    for load in loads:
+    fill_tables(spread_ref, fold_ref)
+    for load in loads[:2]:
         load.wait()
     for c in range(NODES_C):
         stage_a[c * 8 : c * 8 + 8, :] = fields[pl.ds(c, 8, stride=PLANE), :]
@@ -212,6 +244,8 @@
         def _():
             copy.start()
 
+    for load in loads[2:9]:
+        load.wait()
     rows = lax.broadcasted_iota(jnp.int32, (256, 256), 0)
     placing = jnp.where(cell_ref[0:1, :] == rows, 1.0, 0.0).astype(bf16)
 
@@ -225,8 +259,18 @@
     pad = jnp.zeros((3, 256), f32)
     density = jnp.concatenate([density, pad], axis=0)
     modulus = jnp.concatenate([modulus, pad], axis=0)
-    stiff[...] = dot_right(expand_ref[...], density)
-    picked = dot_right(select_ref[...], modulus)
+    expand = ones_where(iota((1024, 128), 0) >> 3 == iota((1024, 128), 1))
+    stiff[...] = dot_right(expand, density)
+    mass_row, node_lane = iota((48, 128), 0), iota((48, 128), 1)
+    select = jnp.concatenate(
+        [
+            ones_where(5 * (mass_row - 20 * ea) + r == node_lane)
+            for r in range(5)
+            for ea in range(2)
+        ],
+        axis=0,
+    )
+    picked = dot_right(select, modulus)
     for r in range(5):
         mass_lhs[:, r * 128 : (r + 1) * 128] = (
             picked[r * 96 : r * 96 + 48, 0:128] + picked[r * 96 + 48 : r * 96 + 96, 128:256]
@@ -249,7 +293,7 @@
     digit_rows = lax.broadcasted_iota(jnp.int32, (16, 256), 0)
     digits = jnp.zeros((16, 256), f32)
     for t in range(4):
-        live = slots < count_ref[0, t]
+        live = slots < count_ref[0:1, t : t + 1]
         number = jnp.where(live, brick_ref[t : t + 1, :] + 1, 0)
         pair = jnp.where(
             digit_rows == 2 * t,
@@ -258,7 +302,9 @@
         )
         listed = jnp.where(elem_ref[t : t + 1, :] == rows, 1.0, 0.0).astype(bf16)
         digits = digits + dot_rows(pair.astype(f32).astype(bf16), listed)
-    own_block[128:144, :] = dot_rows(digits.astype(bf16), placing)
+    digits = dot_rows(digits.astype(bf16), placing)
+    for ea in range(2):
+        blocks_ref[0, ea, 128:144, :] = digits[:, ea * 128 : ea * 128 + 128]
 
     zeros = jnp.zeros((8, 128), f32)
     lhs[360:384, :] = jnp.zeros((24, 512), f32)
@@ -309,11 +355,36 @@
     lax.fori_loop(0, 3, spread_rows, 0)
     product[1000:1024, :] = jnp.zeros((24, 256), f32)
 
+    gather = ones_where(iota((128, 1024), 1) >> 3 == iota((128, 1024), 0), 0.5)
+
     def mates(g):
         return g * pltpu.roll(g, 4, 0)
 
     def eight(k):
         return pl.ds(pl.multiple_of(k * 8, 8), 8)
+
+    def block_send(ea, k):
+        own = 1 if k == 2 else 0
+        return remote(
+            blocks_ref.at[own, ea], blocks_ref.at[1 + k, ea], 3 + 3 * ea + k, up[1 if k else 0]
+        )
+
+    for k in range(3):
+
+        @pl.when(jnp.logical_not(down[k][2]))
+        def _():
+            blocks_ref[1 + k] = jnp.zeros((2, BLOCK_ROWS, 128), f32)
+
+    relayed = below_s & above_d
+
+    def relay(ea):
+        @pl.when(below_s)
+        def _():
+            block_send(ea, 0).wait_recv()
+
+        @pl.when(relayed)
+        def _():
+            block_send(ea, 2).start()
 
     for ea in range(2):
         half = slice(ea * 128, ea * 128 + 128)
@@ -357,21 +428,14 @@
 
         lax.fori_loop(0, 5, line, 0)
 
-    own_block[0:128, :] = dot_right(gather_ref[...], product[...]) * (
-        -time_step * jnp.concatenate([scale_ref[...]] * 2, axis=1)
-    )
-    sends = [remote(own_block, got_blocks.at[k], 3 + k, up[k]) for k in range(3)]
-    for copy, (_, _, there) in zip(sends, up):
-
-        @pl.when(there)
-        def _():
-            copy.start()
-
-    for k in range(3):
-
-        @pl.when(jnp.logical_not(down[k][2]))
-        def _():
-            got_blocks[k] = jnp.zeros((BLOCK_ROWS, 256), f32)
+        blocks_ref[0, ea, 0:128, :] = dot_right(gather, product[:, half]) * (
+            -time_step * scale_ref[...]
+        )
+        for k in range(2):
+
+            @pl.when(up[k][2])
+            def _():
+                block_send(ea, k).start()
 
     forces[160:200, :] += forces[200:240, :]
 
@@ -400,9 +464,9 @@
     face_d[0:8, :] = node(8, 16)
     face_d[8:16, :] = jnp.broadcast_to(mass_sum[208:209, :], (8, 128))
     faces = [
-        remote(face_a, got_a, 6, up[0]),
-        remote(face_c, got_c, 7, up[1]),
-        remote(face_d, got_d, 8, up[2]),
+        remote(face_a, got_a, 9, up[0]),
+        remote(face_c, got_c, 10, up[1]),
+        remote(face_d, got_d, 11, up[2]),
     ]
     for copy, (_, _, there) in zip(faces, up):
 
@@ -416,12 +480,32 @@
         def _():
             buffer[...] = jnp.zeros(buffer.shape, f32)
 
+    relay(0)
+
+    def into_bricks(t):
+        block = jnp.concatenate([blocks_ref[t, 0], blocks_ref[t, 1]], axis=1)
+        stacked = jnp.concatenate(two_terms(block[0:128]), axis=0)
+        row = 128 + 2 * t
+        target = block[row : row + 1] * 32.0 + block[row + 1 : row + 2] - 1.0
+        for n in range(bricks.shape[1] // 256):
+            part = dot_rows(stacked, ones_where(target == (rows + n * 256).astype(f32)))
+            part = part[0:125] + part[128:253]
+            lanes = slice(n * 256, n * 256 + 256)
+            if t == 0:
+                bricks[:, lanes] = part
+            else:
+                bricks[:, lanes] += part
+
     def write_plane(a, carry):
         for c in range(1, NODES_C):
-            force_ref[pl.ds(a * NODES_C + c, 8, stride=PLANE), :] = node(a, c)
+            next_ref[pl.ds(a * NODES_C + c, 8, stride=PLANE), :] = node(a, c)
         return carry
 
     lax.fori_loop(1, NODES_A, write_plane, 0)
+    into_bricks(0)
+    for load in loads[9:]:
+        load.wait()
+    relay(1)
 
     for copy, (_, _, there) in zip(faces, up):
 
@@ -436,35 +520,68 @@
             copy.wait_recv()
 
     for c in range(1, NODES_C):
-        force_ref[pl.ds(c, 8, stride=PLANE), :] = node(0, c) + got_a[c * 8 : c * 8 + 8, :]
+        next_ref[pl.ds(c, 8, stride=PLANE), :] = node(0, c) + got_a[c * 8 : c * 8 + 8, :]
     for a in range(1, NODES_A):
-        force_ref[pl.ds(a * NODES_C, 8, stride=PLANE), :] = (
+        next_ref[pl.ds(a * NODES_C, 8, stride=PLANE), :] = (
             node(a, 0) + got_c[a * 8 : a * 8 + 8, :]
         )
-    force_ref[pl.ds(0, 8, stride=PLANE), :] = (
+    next_ref[pl.ds(0, 8, stride=PLANE), :] = (
         node(0, 0) + got_a[0:8, :] + got_c[0:8, :] + got_d[0:8, :]
     )
     mass_sum[0:16, :] += got_a[128:144, :]
     for a in range(NODES_A):
         mass_sum[a * 24 : a * 24 + 1, :] += got_c[64 + a : 65 + a, :]
     mass_sum[0:1, :] += got_d[8:9, :]
-    for a in range(NODES_A):
-        mass_ref[a * 16 : a * 16 + 16, :] = mass_sum[a * 24 : a * 24 + 16, :]
-
-    for copy, (_, _, there) in zip(sends, up):
-
-        @pl.when(there)
-        def _():
-            copy.wait_send()
-
-    blocks_ref[0] = own_block[...]
-    for k, (copy, (_, _, there)) in enumerate(zip(sends, down)):
-
-        @pl.when(there)
-        def _():
-            copy.wait_recv()
-
-        blocks_ref[1 + k] = got_blocks[k]
+    inverse = jnp.concatenate([mass_sum[a * 24 : a * 24 + 16, :] for a in range(NODES_A)], axis=0)
+    inverse = time_step * time_step / inverse
+
+    def update(x, carry):
+        at = pl.ds(pl.multiple_of(x * PLANE, PLANE), PLANE)
+        next_ref[at, :] = (
+            2.0 * fields[at, :] - old[at, :] + (driven[at, :] - next_ref[at, :]) * inverse
+        )
+        return carry
+
+    lax.fori_loop(0, 8, update, 0)
+
+    writes = [
+        pltpu.make_async_copy(next_ref.at[first], wave_out, write_sem.at[0]),
+        pltpu.make_async_copy(next_ref.at[second], adj_out, write_sem.at[1]),
+        pltpu.make_async_copy(bricks, brick_out, write_sem.at[2]),
+    ]
+    for write in writes[:2]:
+        write.start()
+    into_bricks(1)
+    for k in (1, 2):
+        for ea in range(2):
+
+            @pl.when(down[k][2])
+            def _():
+                block_send(ea, k).wait_recv()
+
+        into_bricks(1 + k)
+    writes[2].start()
+    for ea in range(2):
+        for k, sent in enumerate((above_s, above_d, relayed)):
+
+            @pl.when(sent)
+            def _():
+                block_send(ea, k).wait_send()
+
+    for write in writes:
+        write.wait()
+
+
+def hand_over(*refs):
+    sources, targets, sem = refs[:3], refs[3:6], refs[6]
+    copies = [
+        pltpu.make_async_copy(source, target, sem.at[k])
+        for k, (source, target) in enumerate(zip(sources, targets))
+    ]
+    for copy in copies:
+        copy.start()
+    for copy in copies:
+        copy.wait()
 
 
 def per_device(
@@ -483,20 +600,46 @@
     send_brick,
     send_count,
 ):
-    constants, scale = tables()
-    vmem = pl.BlockSpec(memory_space=pltpu.VMEM)
+    scale = cubature_rows()
     anywhere = pl.BlockSpec(memory_space=pl.ANY)
-    smem = pl.BlockSpec(memory_space=pltpu.SMEM)
-    force, mass, blocks = pl.pallas_call(
+
+    def flat(x):
+        return x.reshape(4 * PLANE, 128)
+
+    operands = [
+        flat(wave_now),
+        flat(adj_now),
+        element_cell,
+        send_elem[0],
+        send_brick[0],
+        send_count,
+        inv_density,
+        inv_modulus,
+        jnp.asarray(scale, f32),
+        flat(wave_old),
+        flat(adj_old),
+        flat(source),
+        flat(adj_source),
+    ]
+    held = [pltpu.VMEM(x.shape, x.dtype) for x in operands[2:9]]
+    half = jax.ShapeDtypeStruct((4 * PLANE, 128), f32)
+    results = (half, half, jax.ShapeDtypeStruct((125, 1024), f32))
+    results_here = pl.pallas_call(
         functools.partial(body, n_surf, n_depth),
-        out_shape=(
-            jax.ShapeDtypeStruct((8 * PLANE, 128), f32),
-            jax.ShapeDtypeStruct((PLANE, 128), f32),
-            jax.ShapeDtypeStruct((4, BLOCK_ROWS, 256), f32),
-        ),
-        in_specs=[anywhere] * 2 + [vmem] * 5 + [smem] + [vmem] * 6,
-        out_specs=(vmem,) * 3,
+        out_shape=results,
+        in_specs=[anywhere] * len(operands),
+        out_specs=(anywhere,) * 3,
         scratch_shapes=[
+            pltpu.VMEM((8 * PLANE, 128), f32),
+            pltpu.VMEM((4, 2, BLOCK_ROWS, 128), f32),
+            pltpu.VMEM((125, 1024), f32),
+            pltpu.VMEM((8 * PLANE, 128), f32),
+        ]
+        + held
+        + [
+            pltpu.VMEM((640, 512), bf16),
+            pltpu.VMEM((512, 640), bf16),
+            pltpu.VMEM((8 * PLANE, 128), f32),
             pltpu.VMEM((8 * PLANE, 128), f32),
             pltpu.VMEM((128, 128), f32),
             pltpu.VMEM((64, 128), f32),
@@ -505,7 +648,7 @@
             pltpu.VMEM((64, 128), f32),
             pltpu.VMEM((384, 512), f32),
             pltpu.VMEM((384, 640), f32),
-            pltpu.VMEM((1000, 256), f32),
+            pltpu.VMEM((1024, 256), f32),
             pltpu.VMEM((1024, 256), f32),
             pltpu.VMEM((400, 640), f32),
             pltpu.VMEM((360, 512), f32),
@@ -518,42 +661,25 @@
             pltpu.VMEM((FACE_A, 128), f32),
             pltpu.VMEM((FACE_C, 128), f32),
             pltpu.VMEM((FACE_D, 128), f32),
-            pltpu.VMEM((BLOCK_ROWS, 256), f32),
-            pltpu.VMEM((3, BLOCK_ROWS, 256), f32),
-            pltpu.SemaphoreType.DMA((2,)),
-            pltpu.SemaphoreType.DMA((9,)),
-            pltpu.SemaphoreType.DMA((9,)),
+            pltpu.SemaphoreType.DMA((3,)),
+            pltpu.SemaphoreType.DMA((len(operands),)),
+            pltpu.SemaphoreType.DMA((12,)),
+            pltpu.SemaphoreType.DMA((12,)),
         ],
         compiler_params=pltpu.CompilerParams(
-            collective_id=0, has_side_effects=True, vmem_limit_bytes=40 * 1024 * 1024
+            collective_id=0, has_side_effects=True, vmem_limit_bytes=60 * 1024 * 1024
         ),
-    )(
-        wave_now.reshape(4 * PLANE, 128),
-        adj_now.reshape(4 * PLANE, 128),
-        inv_density,
-        inv_modulus,
-        element_cell,
-        send_elem[0],
-        send_brick[0],
-        send_count,
-        *[jnp.asarray(c, bf16) for c in constants],
-        jnp.asarray(scale, f32),
-    )
-    force = force.reshape(8, NODES_A, NODES_C, 128)
-    mass = mass.reshape(1, NODES_A, NODES_C, 128)
-    step_square = time_step * time_step
-    wave_next = 2.0 * wave_now - wave_old + step_square * (source - force[:4]) / mass
-    adj_next = 2.0 * adj_now - adj_old + step_square * (adj_source - force[4:]) / mass
-    brick_dev = 1024
-    brick_ids = jnp.arange(brick_dev, dtype=jnp.int32).astype(f32)
-    brick_kernel = 0.0
-    for t in range(4):
-        targets = blocks[t, 128 + 2 * t] * 32.0 + blocks[t, 129 + 2 * t] - 1.0
-        selector = (targets[:, None] == brick_ids[None, :]).astype(f32)
-        brick_kernel = brick_kernel + jnp.dot(
-            blocks[t, :125], selector, precision=precise, preferred_element_type=f32
-        )
-    return wave_next, adj_next, brick_kernel
+    )(*operands)
+    wave_next, adj_next, brick_kernel = pl.pallas_call(
+        hand_over,
+        out_shape=results,
+        in_specs=[anywhere] * 3,
+        out_specs=(anywhere,) * 3,
+        scratch_shapes=[pltpu.SemaphoreType.DMA((3,))],
+        compiler_params=pltpu.CompilerParams(vmem_limit_bytes=60 * 1024 * 1024),
+    )(*results_here)
+    shape = wave_now.shape
+    return wave_next.reshape(shape), adj_next.reshape(shape), brick_kernel
 
 
 def solution(mesh):

time: 38.7 us -> 52.4 us (1.35)
  Pallas kernels: 21.6 us -> 51.6 us
  local copies, waits for them, and re-layouts: 12 us -> 0 us
  matrix products: 2.93 us -> 0 us
  other arithmetic: 0.95 us -> 0 us
    pallas_call x1 -> x2, Pallas kernels: 21.6 us -> 51.6 us  [the longest x1 32.9 us: per_device(): pl.pallas_call(hand_over, out_shape=results, in_specs=[anywhere] * 3, out...]
    unnamed x36 -> x0, local copies, waits for them, and re-layouts: 12 us -> none
    dot_general x4 -> x0, matrix products: 2.93 us -> none  [per_device(): jnp.dot(blocks[t, :125], selector, precision=precise, preferred_element_t...]
    add x1 -> x0, other arithmetic: 0.93 us -> none  [per_device(): 2.0 * adj_now - adj_old + step_square * (adj_source - force[4:]) / mass]
where the time goes in v1:
time: 52.4 us; the launch traced here: 52.2 us
  Pallas kernels  51.6 us (98%)
  between operations  0.64 us (1%)
    pallas_call x1, Pallas kernels, per_device(): pl.pallas_call(hand_over, out_shape=results, in_specs=[anywhere] * 3, out...  32.9 us
    pallas_call x1, Pallas kernels, per_device(): pl.pallas_call(functools.partial(body, n_surf, n_depth), out_shape=result...  18.7 us

profile of v1, /device:TPU:9, one launch (start us, length us, event | category | flops | bytes accessed | tf_op | source)
XLA Modules:
  0.0 52.2 jit_solution(9529030867918013763)
XLA Ops:
  0.6 18.7 %shard_map.148 = (f32[512,128]{1,0:T(8,128)}, f32[512,128]{1,0:T(8,128)}, f32[125,1024]{1,0:T(8,128)}) custom-call(f32[512,128]{1,0:T(8,128)} %bitcast.10, f32[512,128]{1,0:T(8,128)} %bitcast.11, s32[1,256]{1,0:T(1,128)} %cell_hbm.1, s32[4,256]{1,0:T(4,128)} %bitcast.16, s32[4,256]{1,0:T(4,128)} %bitcast.17, s32[1,4]{1,0:T(1,128)} %count_hbm.1, ...), custom_call_target="tpu_custom_call" | custom-call | tf_op jit(solution)/shard_map/pallas_call | solution.py:627
  19.3 32.9 %shard_map.149 = (f32[512,128]{1,0:T(8,128)}, f32[512,128]{1,0:T(8,128)}, f32[125,1024]{1,0:T(8,128)}) custom-call(f32[512,128]{1,0:T(8,128)} %get-tuple-element.9.refs_0_, f32[512,128]{1,0:T(8,128)} %get-tuple-element.10.refs_1_, f32[125,1024]{1,0:T(8,128)} %get-tuple-element.11.refs_2_), custom_call_target="tpu_custom_call" | custom-call | tf_op jit(solution)/shard_map/pallas_call | solution.py:673

commit v2 on v1

--- a/solution.py
+++ b/solution.py
@@ -68,10 +68,8 @@
 
 
 def dot_left(x, table):
-    high, low = two_terms(x)
-    return jnp.dot(high, table, preferred_element_type=f32) + jnp.dot(
-        low, table, preferred_element_type=f32
-    )
+    both = jnp.dot(jnp.concatenate(two_terms(x), axis=0), table, preferred_element_type=f32)
+    return both[: x.shape[0]] + both[x.shape[0] :]
 
 
 def dot_right(table, x):
@@ -308,6 +306,7 @@
 
     zeros = jnp.zeros((8, 128), f32)
     lhs[360:384, :] = jnp.zeros((24, 512), f32)
+    forces[200:384, :] = jnp.zeros((184, 640), f32)
 
     def place(a, c, tile):
         ec, q = c // 4, c % 4
@@ -347,12 +346,7 @@
         place(a, 16, halo_c[a * 8 : a * 8 + 8, :])
     place(8, 16, halo_d[...])
 
-    def spread_rows(k, carry):
-        at = pl.ds(pl.multiple_of(k * 128, 128), 128)
-        values[at, :] = dot_left(lhs[at, :], spread_ref[...])
-        return carry
-
-    lax.fori_loop(0, 3, spread_rows, 0)
+    values[...] = dot_left(lhs[...], spread_ref[...])
     product[1000:1024, :] = jnp.zeros((24, 256), f32)
 
     gather = ones_where(iota((128, 1024), 1) >> 3 == iota((128, 1024), 0), 0.5)
@@ -411,7 +405,9 @@
                 f = backward([k[q][r] * g[r] for r in range(5)])
                 for r in range(5):
                     product[eight(p * 25 + q * 5 + r), half] = pair[q][r] + mates(g[r])
-                    forces[eight(ea * 25 + p * 5 + q), r * 128 : r * 128 + 128] = force[q][r] + f[r]
+                    at = eight((4 * ea + p) * 5 + q), slice(r * 128, r * 128 + 128)
+                    total = force[q][r] + f[r]
+                    forces[at] = total if ea == 0 else forces[at] + total
             return carry
 
         lax.fori_loop(0, 5, plane, 0)
@@ -423,7 +419,7 @@
                 f = backward([stiff[eight(p * 25 + q * 5 + r), half] * g[p] for p in range(5)])
                 for p in range(5):
                     product[eight(p * 25 + q * 5 + r), half] += mates(g[p])
-                    forces[eight(ea * 25 + p * 5 + q), lanes] += f[p]
+                    forces[eight((4 * ea + p) * 5 + q), lanes] += f[p]
             return carry
 
         lax.fori_loop(0, 5, line, 0)
@@ -437,13 +433,7 @@
             def _():
                 block_send(ea, k).start()
 
-    forces[160:200, :] += forces[200:240, :]
-
-    def fold_rows(first, count, at):
-        folded[at : at + count, :] = dot_left(forces[first : first + count, :], fold_ref[...])
-
-    fold_rows(0, 200, 0)
-    fold_rows(240, 160, 200)
+    folded[...] = dot_left(forces[...], fold_ref[...])
 
     def node(a, c):
         ec, q = c // 4, c % 4
@@ -482,6 +472,13 @@
 
     relay(0)
 
+    def arrived(k):
+        for ea in range(2):
+
+            @pl.when(down[k][2])
+            def _():
+                block_send(ea, k).wait_recv()
+
     def into_bricks(t):
         block = jnp.concatenate([blocks_ref[t, 0], blocks_ref[t, 1]], axis=1)
         stacked = jnp.concatenate(two_terms(block[0:128]), axis=0)
@@ -506,6 +503,9 @@
     for load in loads[9:]:
         load.wait()
     relay(1)
+    into_bricks(1)
+    arrived(1)
+    into_bricks(2)
 
     for copy, (_, _, there) in zip(faces, up):
 
@@ -551,15 +551,8 @@
     ]
     for write in writes[:2]:
         write.start()
-    into_bricks(1)
-    for k in (1, 2):
-        for ea in range(2):
-
-            @pl.when(down[k][2])
-            def _():
-                block_send(ea, k).wait_recv()
-
-        into_bricks(1 + k)
+    arrived(2)
+    into_bricks(3)
     writes[2].start()
     for ea in range(2):
         for k, sent in enumerate((above_s, above_d, relayed)):
@@ -573,15 +566,22 @@
 
 
 def hand_over(*refs):
-    sources, targets, sem = refs[:3], refs[3:6], refs[6]
-    copies = [
-        pltpu.make_async_copy(source, target, sem.at[k])
-        for k, (source, target) in enumerate(zip(sources, targets))
+    sources, targets, held, sem = refs[:3], refs[3:6], refs[6:9], refs[9]
+    loads = [
+        pltpu.make_async_copy(source, mine, sem.at[k])
+        for k, (source, mine) in enumerate(zip(sources, held))
     ]
-    for copy in copies:
-        copy.start()
-    for copy in copies:
-        copy.wait()
+    stores = [
+        pltpu.make_async_copy(mine, target, sem.at[3 + k])
+        for k, (mine, target) in enumerate(zip(held, targets))
+    ]
+    for load in loads:
+        load.start()
+    for load, store in zip(loads, stores):
+        load.wait()
+        store.start()
+    for store in stores:
+        store.wait()
 
 
 def per_device(
@@ -650,8 +650,8 @@
             pltpu.VMEM((384, 640), f32),
             pltpu.VMEM((1024, 256), f32),
             pltpu.VMEM((1024, 256), f32),
-            pltpu.VMEM((400, 640), f32),
-            pltpu.VMEM((360, 512), f32),
+            pltpu.VMEM((384, 640), f32),
+            pltpu.VMEM((384, 512), f32),
             pltpu.VMEM((48, 640), f32),
             pltpu.VMEM((48, 512), f32),
             pltpu.VMEM((216, 128), f32),
@@ -675,7 +675,8 @@
         out_shape=results,
         in_specs=[anywhere] * 3,
         out_specs=(anywhere,) * 3,
-        scratch_shapes=[pltpu.SemaphoreType.DMA((3,))],
+        scratch_shapes=[pltpu.VMEM(x.shape, f32) for x in results]
+        + [pltpu.SemaphoreType.DMA((6,))],
         compiler_params=pltpu.CompilerParams(vmem_limit_bytes=60 * 1024 * 1024),
     )(*results_here)
     shape = wave_now.shape

time: 52.4 us -> 20.7 us (0.40)
  Pallas kernels: 51.6 us -> 19.9 us
    pallas_call x1, Pallas kernels: 32.9 us -> 2.05 us  [per_device(): pl.pallas_call(hand_over, out_shape=results, in_specs=[anywhere] * 3, out...]
    pallas_call x1, Pallas kernels: 18.7 us -> 17.9 us  [per_device(): pl.pallas_call(functools.partial(body, n_surf, n_depth), out_shape=result...]
where the time goes in v2:
time: 20.7 us; the launch traced here: 20.6 us
  Pallas kernels  19.9 us (96%)
  between operations  0.64 us (3%)
    pallas_call x1, Pallas kernels, per_device(): pl.pallas_call(functools.partial(body, n_surf, n_depth), out_shape=result...  17.9 us
    pallas_call x1, Pallas kernels, per_device(): pl.pallas_call(hand_over, out_shape=results, in_specs=[anywhere] * 3, out...  2.05 us

profile of v2, /device:TPU:9, one launch (start us, length us, event | category | flops | bytes accessed | tf_op | source)
XLA Modules:
  0.0 20.6 jit_solution(1017515711344443138)
XLA Ops:
  0.6 17.9 %shard_map.148 = (f32[512,128]{1,0:T(8,128)}, f32[512,128]{1,0:T(8,128)}, f32[125,1024]{1,0:T(8,128)}) custom-call(f32[512,128]{1,0:T(8,128)} %bitcast.10, f32[512,128]{1,0:T(8,128)} %bitcast.11, s32[1,256]{1,0:T(1,128)} %cell_hbm.1, s32[4,256]{1,0:T(4,128)} %bitcast.16, s32[4,256]{1,0:T(4,128)} %bitcast.17, s32[1,4]{1,0:T(1,128)} %count_hbm.1, ...), custom_call_target="tpu_custom_call" | custom-call | tf_op jit(solution)/shard_map/pallas_call | solution.py:627
  18.5 2.0 %shard_map.149 = (f32[512,128]{1,0:T(8,128)}, f32[512,128]{1,0:T(8,128)}, f32[125,1024]{1,0:T(8,128)}) custom-call(f32[512,128]{1,0:T(8,128)} %get-tuple-element.9.refs_0_, f32[512,128]{1,0:T(8,128)} %get-tuple-element.10.refs_1_, f32[125,1024]{1,0:T(8,128)} %get-tuple-element.11.refs_2_), custom_call_target="tpu_custom_call" | custom-call | tf_op jit(solution)/shard_map/pallas_call | solution.py:673

commit v3 on v2

--- a/solution.py
+++ b/solution.py
@@ -565,25 +565,6 @@
         write.wait()
 
 
-def hand_over(*refs):
-    sources, targets, held, sem = refs[:3], refs[3:6], refs[6:9], refs[9]
-    loads = [
-        pltpu.make_async_copy(source, mine, sem.at[k])
-        for k, (source, mine) in enumerate(zip(sources, held))
-    ]
-    stores = [
-        pltpu.make_async_copy(mine, target, sem.at[3 + k])
-        for k, (mine, target) in enumerate(zip(held, targets))
-    ]
-    for load in loads:
-        load.start()
-    for load, store in zip(loads, stores):
-        load.wait()
-        store.start()
-    for store in stores:
-        store.wait()
-
-
 def per_device(
     n_surf,
     n_depth,
@@ -624,7 +605,7 @@
     held = [pltpu.VMEM(x.shape, x.dtype) for x in operands[2:9]]
     half = jax.ShapeDtypeStruct((4 * PLANE, 128), f32)
     results = (half, half, jax.ShapeDtypeStruct((125, 1024), f32))
-    results_here = pl.pallas_call(
+    wave_next, adj_next, brick_kernel = pl.pallas_call(
         functools.partial(body, n_surf, n_depth),
         out_shape=results,
         in_specs=[anywhere] * len(operands),
@@ -670,15 +651,6 @@
             collective_id=0, has_side_effects=True, vmem_limit_bytes=60 * 1024 * 1024
         ),
     )(*operands)
-    wave_next, adj_next, brick_kernel = pl.pallas_call(
-        hand_over,
-        out_shape=results,
-        in_specs=[anywhere] * 3,
-        out_specs=(anywhere,) * 3,
-        scratch_shapes=[pltpu.VMEM(x.shape, f32) for x in results]
-        + [pltpu.SemaphoreType.DMA((6,))],
-        compiler_params=pltpu.CompilerParams(vmem_limit_bytes=60 * 1024 * 1024),
-    )(*results_here)
     shape = wave_now.shape
     return wave_next.reshape(shape), adj_next.reshape(shape), brick_kernel
 

time: 20.7 us -> 21.9 us (1.058)
  local copies, waits for them, and re-layouts: 0 us -> 3.25 us
  Pallas kernels: 19.9 us -> 17.9 us
    unnamed x0 -> x7, local copies, waits for them, and re-layouts: none -> 3.25 us
    pallas_call x1 -> x0, Pallas kernels: 2.05 us -> none  [per_device(): pl.pallas_call(hand_over, out_shape=results, in_specs=[anywhere] * 3, out...]
where the time goes in v3:
time: 21.9 us; the launch traced here: 21.8 us
  Pallas kernels  17.9 us (82%)
  local copies, waits for them, and re-layouts  3.25 us (15%)
  between operations  0.66 us (3%)
    pallas_call x1, Pallas kernels, per_device(): pl.pallas_call(functools.partial(body, n_surf, n_depth), out_shape=result...  17.9 us
    unnamed x7, local copies, waits for them, and re-layouts  3.25 us

profile of v3, /device:TPU:9, one launch (start us, length us, event | category | flops | bytes accessed | tf_op | source)
XLA Modules:
  0.0 21.8 jit_solution(1610422722155029213)
XLA Ops:
  0.6 17.9 %shard_map.148 = (f32[512,128]{1,0:T(8,128)}, f32[512,128]{1,0:T(8,128)}, f32[125,1024]{1,0:T(8,128)}) custom-call(f32[512,128]{1,0:T(8,128)} %bitcast.12, f32[512,128]{1,0:T(8,128)} %bitcast.13, s32[1,256]{1,0:T(1,128)} %cell_hbm.1, s32[4,256]{1,0:T(4,128)} %bitcast.18, s32[4,256]{1,0:T(4,128)} %bitcast.19, s32[1,4]{1,0:T(1,128)} %count_hbm.1, ...), custom_call_target="tpu_custom_call" | custom-call | tf_op jit(solution)/shard_map/pallas_call | solution.py:608
  18.5 0.0 copy-start.1
  18.5 0.0 copy-start
  18.5 1.7 %copy.19 = f32[4,8,16,128]{3,2,1,0:T(8,128)} copy(f32[4,8,16,128]{3,2,1,0:T(8,128)} %bitcast.11) | data formatting | bytes 524288
  20.3 0.0 copy-done.1
  20.3 0.7 %copy.20 = f32[4,8,16,128]{3,2,1,0:T(8,128)} copy(f32[4,8,16,128]{3,2,1,0:T(8,128)S(1)} %bitcast.10) | data formatting | bytes 524288
  21.0 0.0 copy-done
  21.0 0.8 %copy.21 = f32[125,1024]{1,0:T(8,128)} copy(f32[125,1024]{1,0:T(8,128)S(1)} %copy-done) | data formatting | bytes 1024000
Async XLA Ops:
  18.5 1.8 %copy-start.1 = (f32[512,128]{1,0:T(8,128)S(1)}, f32[512,128]{1,0:T(8,128)}, u32[]{:S(2)}) copy-start(f32[512,128]{1,0:T(8,128)} %get-tuple-element.7) | copy-start | bytes 786436
  18.5 2.5 %copy-start = (f32[125,1024]{1,0:T(8,128)S(1)}, f32[125,1024]{1,0:T(8,128)}, u32[]{:S(2)}) copy-start(f32[125,1024]{1,0:T(8,128)} %get-tuple-element.14) | copy-start | bytes 1536004
